TPU v7x, 512 devices: a whole 4x8x8 slice. The times are simulated.
512 devices in a mesh: dp: 32 (over y_lo, z, core), row: 4 (over y_hi), col: 4 (over x).
Axes of the slice: x: 4, y: 8 (y_hi: 4, y_lo: 2; y = y_hi * 2 + y_lo), z: 8, core: 2. Of those that a mesh axis runs over, the one named last changes fastest.
Arguments:
- heads_out: bfloat16 [8192, 6144], P(('dp', 'col'), 'row'), may hold values from -6 to 6
- residual: bfloat16 [8192, 6144], P('dp', 'col'), may hold values from -6 to 6
- master: float32 [6144, 6144], P(('row', 'dp'), 'col'), may hold values from -6 to 6
- moment_one: float32 [6144, 6144], P(('row', 'dp'), 'col'), may hold values from -4 to 4
- moment_two: float32 [6144, 6144], P(('row', 'dp'), 'col'), may hold values from 0.05 to 2
- out_grad: bfloat16 [8192, 6144], P('dp', 'col'), may hold values from -6 to 6
Outputs:
- stream_out: bfloat16 [8192, 6144], P('dp', 'col')
- heads_grad: bfloat16 [8192, 6144], P(('dp', 'col'), 'row')
- weight_grad: float32 [6144, 6144], P(('row', 'dp'), 'col')
- new_master: float32 [6144, 6144], P(('row', 'dp'), 'col')
- new_moment_one: float32 [6144, 6144], P(('row', 'dp'), 'col')
- new_moment_two: float32 [6144, 6144], P(('row', 'dp'), 'col')
All inputs are finite; a program needn't handle non-finite values.
Results may differ from a plain program's by a relative error of at most 0.009.
Values may be sent and summed in bfloat16 or wider, within the bound.
A program may use at most 64 MiB of HBM per device.

v0:
```python
import math

import jax
import jax.numpy as jnp
from jax import lax
from jax.sharding import PartitionSpec as P

HEADS = 48
HEAD_DIM = 128


beta_one = 0.9
beta_two = 0.95
learn_rate = 0.1
weight_decay = 0.1
epsilon = 1e-08


def filled_up(lines, count):
    spare = -len(lines) % count
    return jnp.pad(lines, [(0, spare)] + [(0, 0)] * (lines.ndim - 1))


def sum_by_parts(shard, axis):
    lines = shard.reshape(-1, *shard.shape[1:][-1:])
    padded = filled_up(lines, lax.axis_size(axis))
    own = lax.psum_scatter(padded, axis, scatter_dimension=0, tiled=True)
    whole = lax.all_gather(own, axis, axis=0, tiled=True)
    return whole[: len(lines)].reshape(shard.shape)


def in_blocks(shard, dim, count):
    before, after = (shard.shape[:dim], shard.shape[dim + 1 :])
    return jnp.moveaxis(shard.reshape(*before, count, -1, *after), dim, 0)


def sent_and_summed(shard, axis, dim):
    count = lax.axis_size(axis)
    tiles = lax.all_to_all(in_blocks(shard, dim, count), axis, 0, 0, tiled=True)
    return jnp.sum(tiles.astype(jnp.float32), axis=0)


def owner_grads(gathered, out_grad, fan_scale):
    tile_grad = (
        lax.dot_general(
            gathered, out_grad, (((0,), (0,)), ((), ())), preferred_element_type=jnp.float32
        )
        * fan_scale
    )
    owners = lax.axis_size("dp")
    stacked = tile_grad.astype(jnp.bfloat16).reshape(
        owners, tile_grad.shape[0] // owners, tile_grad.shape[1]
    )
    received = lax.all_to_all(stacked, "dp", split_axis=0, concat_axis=0, tiled=True)
    return jnp.sum(received.astype(jnp.float32), axis=0)


def shards(heads_out, residual, master, moment_one, moment_two, out_grad):
    fan_scale = 1.0 / math.sqrt(HEADS * HEAD_DIM)
    local_weight = master.astype(jnp.bfloat16)
    gathered = lax.all_gather(heads_out, "col", axis=0, tiled=True)
    weight_grad = None
    weight_tile = lax.all_gather(local_weight, "dp", axis=0, tiled=True)
    partial_sum = jnp.dot(gathered, weight_tile, preferred_element_type=jnp.float32) * fan_scale
    head_terms = (
        lax.dot_general(
            out_grad, weight_tile, (((1,), (1,)), ((), ())), preferred_element_type=jnp.float32
        )
        * fan_scale
    )
    mixed_sum = sum_by_parts(partial_sum.astype(jnp.bfloat16), "row").astype(jnp.float32)
    stream_out = (residual.astype(jnp.float32) + mixed_sum).astype(jnp.bfloat16)
    heads_grad = sent_and_summed(head_terms.astype(jnp.bfloat16), "col", 0).astype(jnp.bfloat16)
    weight_grad = owner_grads(gathered, out_grad, fan_scale)
    new_moment_one = beta_one * moment_one + (1.0 - beta_one) * weight_grad
    new_moment_two = beta_two * moment_two + (1.0 - beta_two) * weight_grad * weight_grad
    bias_one = 1.0 - beta_one**10
    bias_two = 1.0 - beta_two**10
    direction = new_moment_one / bias_one / (jnp.sqrt(new_moment_two / bias_two) + epsilon)
    new_master = master - learn_rate * (direction + weight_decay * master)
    return (stream_out, heads_grad, weight_grad, new_master, new_moment_one, new_moment_two)


def solution(mesh):
    return jax.shard_map(
        shards,
        mesh=mesh,
        in_specs=(
            P(("dp", "col"), "row"),
            P("dp", "col"),
            P(("row", "dp"), "col"),
            P(("row", "dp"), "col"),
            P(("row", "dp"), "col"),
            P("dp", "col"),
        ),
        out_specs=(
            P("dp", "col"),
            P(("dp", "col"), "row"),
            P(("row", "dp"), "col"),
            P(("row", "dp"), "col"),
            P(("row", "dp"), "col"),
            P(("row", "dp"), "col"),
        ),
        check_vma=False,
    )
```

profile of v0, /device:TPU:4, one launch (start us, length us, event | category | flops | bytes accessed | tf_op | source)
XLA Modules:
  0.0 276.4 jit_solution(10970078683171486864)
XLA Ops:
  7.2 0.0 copy-start
  7.2 0.0 all-gather.2.cloned.1.call-start
  7.2 17.5 %all_gather.9 = bf16[256,1536]{1,0:T(8,128)(2,1)S(1)} all-gather(bf16[64,1536]{1,0:T(8,128)(2,1)} %param.6), channel_id=1, replica_groups=mesh['dp'=32,'row'=4,'col'=4] {'col'}, dimensions={0}, use_global_device_ids=true | all-gather | bytes 983040 | tf_op jit(solution)/shard_map/all_gather | solution.py:61
  24.7 0.0 copy-done
  24.7 1.4 fusion
  26.1 113.2 %all_to_all.10 = bf16[32,48,1536]{2,1,0:T(8,128)(2,1)S(1)} all-to-all(bf16[32,48,1536]{2,1,0:T(8,128)(2,1)S(1)} %bitcast.8), channel_id=1, replica_groups=mesh['dp'=32,'row'=4,'col'=4] {'dp'}, dimensions={0} | all-to-all | bytes 9437184 | tf_op jit(solution)/shard_map/all_to_all | solution.py:54
  139.3 0.7 convert_reduce_fusion
  140.0 0.3 copy-done.3
  140.3 0.1 copy-done.4
  140.3 0.1 copy-done.5
  140.4 1.1 multiply_subtract_fusion
  141.6 0.0 all-gather.2.cloned.1.call-update
  141.6 0.0 reduce-scatter.2.cloned.1.call-start
  141.7 69.5 %all-gather.2.cloned.1.call-done = bf16[1536,1536]{1,0:T(8,128)(2,1)} async-done(((bf16[48,1536]{1,0:T(8,128)(2,1)}), bf16[1536,1536]{1,0:T(8,128)(2,1)}) %all-gather.2.cloned.1.call-update) | async-done | bytes 4718608 | tf_op jit(solution)/shard_map/all_gather | solution.py:63
  211.1 4.6 %fusion.1 = bf16[256,1536]{1,0:T(8,128)(2,1)} fusion(bf16[256,1536]{1,0:T(8,128)(2,1)S(1)} %all_gather.9, bf16[1536,1536]{1,0:T(8,128)(2,1)} %all-gather.2.cloned.1.call-done), kind=kOutput, calls=%fused_computation.5 | convolution fusion | flops 1208745984 | bytes 6291456 | tf_op jit(solution)/shard_map/dot_general | solution.py:64
  215.7 0.0 copy-done.1
  215.7 0.0 reduce-scatter.2.cloned.1.call-update
  215.8 0.0 copy-start.2
  215.8 3.8 %fusion.2 = bf16[256,1536]{1,0:T(8,128)(2,1)S(1)} fusion(bf16[256,1536]{1,0:T(8,128)(2,1)S(1)} %copy-done, bf16[1536,1536]{1,0:T(8,128)(2,1)} %all-gather.2.cloned.1.call-done), kind=kOutput, calls=%fused_computation.6 | convolution fusion | flops 1208745984 | bytes 6291456 | tf_op jit(solution)/shard_map/dot_general | solution.py:66
  219.6 14.6 %all_to_all.11 = bf16[4,64,1536]{2,1,0:T(8,128)(2,1)S(1)} all-to-all(bf16[4,64,1536]{2,1,0:T(8,128)(2,1)S(1)} %bitcast.9), channel_id=1, replica_groups=mesh['dp'=32,'row'=4,'col'=4] {'col'}, dimensions={0} | all-to-all | bytes 1572864 | tf_op jit(solution)/shard_map/all_to_all | solution.py:39
  234.2 0.8 reduce_sum.21
  235.0 13.4 %reduce-scatter.2.cloned.1.call-done = bf16[64,1536]{1,0:T(8,128)(2,1)} async-done(((bf16[256,1536]{1,0:T(8,128)(2,1)}), bf16[64,1536]{1,0:T(8,128)(2,1)}) %reduce-scatter.2.cloned.1.call-update) | async-done | bytes 196624 | tf_op jit(solution)/shard_map/reduce_scatter | solution.py:27
  248.4 20.1 %all_gather.11 = bf16[256,1536]{1,0:T(8,128)(2,1)S(1)} all-gather(bf16[64,1536]{1,0:T(8,128)(2,1)} %reduce-scatter.2.cloned.1.call-done), channel_id=1, replica_groups=mesh['dp'=32,'row'=4,'col'=4] {'row'}, dimensions={0}, use_global_device_ids=true | all-gather | bytes 983040 | tf_op jit(solution)/shard_map/all_gather | solution.py:28
  268.5 1.1 add_convert_fusion
  (5 shorter events, 0.0 us)
Async XLA Ops:
  7.2 17.5 %copy-start = (bf16[256,1536]{1,0:T(8,128)(2,1)S(1)}, bf16[256,1536]{1,0:T(8,128)(2,1)}, u32[]{:S(2)}) copy-start(bf16[256,1536]{1,0:T(8,128)(2,1)} %param.11) | copy-start | bytes 2359300
  7.2 203.9 %all-gather.2.cloned.1.call-start = ((), (), s32[]{:S(2)}) async-start(), calls=%async_computation.3 | async-start | bytes 4866048 | tf_op jit(solution)/shard_map/all_gather | solution.py:63
  139.3 1.0 copy-start.3
  139.3 1.0 copy-start.4
  139.3 1.1 copy-start.5
  140.4 75.3 %copy-start.1 = (f32[48,1536]{1,0:T(8,128)}, f32[48,1536]{1,0:T(8,128)S(1)}, u32[]{:S(2)}) copy-start(f32[48,1536]{1,0:T(8,128)S(1)} %convert_reduce_fusion) | copy-start | bytes 884740
  141.6 106.7 %reduce-scatter.2.cloned.1.call-start = ((), (), s32[]{:S(2)}) async-start(), calls=%async_computation.4 | async-start | bytes 983040 | tf_op jit(solution)/shard_map/reduce_scatter | solution.py:27
  215.8 52.8 %copy-start.2 = (bf16[256,1536]{1,0:T(8,128)(2,1)S(1)}, bf16[256,1536]{1,0:T(8,128)(2,1)}, u32[]{:S(2)}) copy-start(bf16[256,1536]{1,0:T(8,128)(2,1)} %param.7) | copy-start | bytes 2359300
Sparse Core Ops, SparseCore 0:
  141.7 69.3 all-gather.1
  215.9 32.4 reduce-scatter.1
where the time goes:
time: 277 us; the launch traced here: 276 us
  blocking collectives  165 us (60%)
  waiting for transfers between devices  82.9 us (30%)
  between operations  14.1 us (5%)
  matrix products  9.84 us (4%)
  other arithmetic  3.7 us (1%)
    all_to_all x1, blocking collectives, owner_grads(): lax.all_to_all(stacked, 'dp', split_axis=0, concat_axis=0, tiled=True)  113 us
    all_gather x1, waiting for transfers between devices, shards(): weight_tile = lax.all_gather(local_weight, 'dp', axis=0, tiled=True)  69.5 us
    all_gather x1, blocking collectives, sum_by_parts(): whole = lax.all_gather(own, axis, axis=0, tiled=True)  20.1 us
    all_gather x1, blocking collectives, shards(): gathered = lax.all_gather(heads_out, 'col', axis=0, tiled=True)  17.5 us
    all_to_all x1, blocking collectives, sent_and_summed(): tiles = lax.all_to_all(in_blocks(shard, dim, count), axis, 0, 0, tiled=True)  14.6 us
    reduce_scatter x1, waiting for transfers between devices, sum_by_parts(): own = lax.psum_scatter(padded, axis, scatter_dimension=0, tiled=True)  13.4 us
  transfers between devices with their start and end apart: 2, of which 2 were waited for; matrix products, arithmetic and copies ran while one was open for 2% of the time, Pallas kernels for 0%

commit v1 on v0

v1 whole, which is shorter than its diff:
```python
import math

import jax
import jax.numpy as jnp
from jax import lax
from jax.experimental import pallas as pl
from jax.experimental.pallas import tpu as pltpu
from jax.sharding import PartitionSpec as P

HEADS = 48
HEAD_DIM = 128

beta_one = 0.9
beta_two = 0.95
learn_rate = 0.1
weight_decay = 0.1
epsilon = 1e-08

MESH = pl.DeviceIdType.MESH
BF16, F32 = jnp.bfloat16, jnp.float32

NX, NY, NZ = 4, 8, 8
TOK = 256
QTOK = 64
KHALF = 768
COLS = 1536
NHALF = 768
ROWS = 48
SIDES = (1, -1)
SCALE = 1.0 / math.sqrt(HEADS * HEAD_DIM)


def reach(part, side, around):
    longer = around // 2
    return longer if (part == 0) == (side == 0) else around - 1 - longer


def kernel(
    h_ref, res_ref, master_ref, m1_ref, m2_ref, g_ref,
    stream_ref, hgrad_ref, wg_ref, nm_ref, n1_ref, n2_ref,
    hbuf, gbuf, wbuf, yp, ysend, yrecv, yout, resv,
    hp, hsend, hrecv, hfin, dwp, dwx_send, dwx_recv, dsend, drecv,
    mv, m1v, m2v, wgv, nmv, n1v, n2v,
    wz_s, wz_r, wc_s, wc_r, hx_s, hx_r, gx_s, gx_r, y_s, y_r, ya_s, ya_r,
    dh_s, dh_r, hy_s, hy_r, dx_s, dx_r, dz_s, dz_r, loc,
):
    dp, yh, x = lax.axis_index("dp"), lax.axis_index("row"), lax.axis_index("col")
    c = lax.rem(dp, 2)
    z = lax.rem(lax.div(dp, 2), NZ)
    yl = lax.div(dp, 2 * NZ)
    y = 2 * yh + yl

    def wrap(v, n):
        return lax.rem(v + n, n)

    def device(dx=0, dy=0, dz=0, flip=False):
        yy = wrap(y + dy, NY)
        core = 1 - c if flip else c
        return ((lax.rem(yy, 2) * NZ + wrap(z + dz, NZ)) * 2 + core, lax.div(yy, 2), wrap(x + dx, NX))

    to_partner = 1 - 2 * yl
    zdev = [device(dz=s) for s in SIDES]
    xdev = [device(dx=s) for s in SIDES]
    ydev = [device(dy=s) for s in SIDES]
    y2dev = [device(dy=2 * s) for s in SIDES]
    cdev = device(flip=True)
    pdev = device(dy=to_partner)
    hidev = device(dy=-to_partner)

    sent = []

    def remote(src, dst, ssem, rsem, dev):
        return pltpu.make_async_remote_copy(
            src_ref=src, dst_ref=dst, send_sem=ssem, recv_sem=rsem, device_id=dev, device_id_type=MESH)

    def send(src, dst, ssem, rsem, dev):
        copy = remote(src, dst, ssem, rsem, dev)
        copy.start()
        sent.append(copy)

    def arrived(dst, ssem, rsem, dev):
        remote(dst, dst, ssem, rsem, dev).wait_recv()

    def own_cols(v):
        return pl.ds(pl.multiple_of(v * KHALF, KHALF), KHALF)

    load_master = pltpu.make_async_copy(master_ref, mv, loc.at[0])
    load_master.start()
    load_h = pltpu.make_async_copy(h_ref.at[:, own_cols(yl)], hbuf.at[yl * NX + x], loc.at[1])
    load_h.start()
    load_g = pltpu.make_async_copy(g_ref, gbuf.at[pl.ds(pl.multiple_of(yl * TOK, TOK), TOK)], loc.at[2])
    load_g.start()
    load_res = pltpu.make_async_copy(
        res_ref.at[pl.ds(pl.multiple_of(yh * QTOK, QTOK), QTOK)], resv, loc.at[3])
    load_res.start()
    load_m1 = pltpu.make_async_copy(m1_ref, m1v, loc.at[4])
    load_m1.start()
    load_m2 = pltpu.make_async_copy(m2_ref, m2v, loc.at[5])
    load_m2.start()

    barrier = pltpu.get_barrier_semaphore()
    around = zdev + xdev + ydev + y2dev + [cdev]
    for dev in around:
        pl.semaphore_signal(barrier, inc=1, device_id=dev, device_id_type=MESH)
    load_master.wait()
    own = z * 2 + c
    for nh in range(2):
        wbuf[nh, own] = mv[:, nh * NHALF:(nh + 1) * NHALF].astype(BF16)
    pl.semaphore_wait(barrier, len(around))

    def wz_send(nh, side, s):
        slot = wbuf.at[nh, wrap(z - SIDES[side] * s, NZ) * 2 + c]
        send(slot, slot, wz_s.at[nh, side, s], wz_r.at[nh, side, s], zdev[side])

    def wc_send(nh, k, zz):
        slot = wbuf.at[nh, zz * 2 + c]
        send(slot, slot, wc_s.at[nh, k], wc_r.at[nh, k], cdev)

    def wz_step(nh, s):
        for side in range(2):
            if s <= reach(nh, side, NZ):
                zz = wrap(z - SIDES[side] * s, NZ)
                arrived(wbuf.at[nh, zz * 2 + c], wz_s.at[nh, side, s - 1], wz_r.at[nh, side, s - 1], zdev[side])
                if s < reach(nh, side, NZ):
                    wz_send(nh, side, s)
                wc_send(nh, s if side == 0 else reach(nh, 0, NZ) + s, zz)

    def wc_wait(nh):
        for k in range(NZ):
            up = reach(nh, 0, NZ)
            zz = z if k == 0 else wrap(z - k, NZ) if k <= up else wrap(z + (k - up), NZ)
            arrived(wbuf.at[nh, zz * 2 + 1 - c], wc_s.at[nh, k], wc_r.at[nh, k], cdev)

    other = 1 - yl

    def hx_send(src, slot, k, dev):
        send(src, hbuf.at[slot], hx_s.at[k], hx_r.at[k], dev)

    def h_arrived(slot, k):
        arrived(hbuf.at[slot], hx_s.at[k], hx_r.at[k], pdev)

    for side in range(2):
        wz_send(0, side, 0)
    hx_send(h_ref.at[:, own_cols(other)], yl * NX + x, 0, pdev)
    for side in range(2):
        hx_send(h_ref.at[:, own_cols(yl)], yl * NX + x, 1 + side, xdev[side])
    half = TOK // 2
    g_first = pl.ds(pl.multiple_of(other * half, half), half)
    g_there = pl.ds(pl.multiple_of(yl * TOK + other * half, half), half)
    send(g_ref.at[g_first], gbuf.at[g_there], gx_s.at[0], gx_r.at[0], hidev)
    wc_send(0, 0, z)
    for side in range(2):
        wz_send(1, side, 0)
    wc_send(1, 0, z)

    h_arrived(other * NX + x, 0)
    for side in range(2):
        hx_send(hbuf.at[other * NX + x], other * NX + x, 3 + side, xdev[side])
    g_last = pl.ds(pl.multiple_of(yl * half, half), half)
    g_goal = pl.ds(pl.multiple_of(yl * TOK + yl * half, half), half)
    send(g_ref.at[g_last], gbuf.at[g_goal], gx_s.at[1], gx_r.at[1], pdev)

    wz_step(0, 1)
    for side in range(2):
        h_arrived(yl * NX + wrap(x - SIDES[side], NX), 1 + side)
    for side in range(2):
        h_arrived(other * NX + wrap(x - SIDES[side], NX), 3 + side)
    for g in range(2):
        slot = g * NX + wrap(x - SIDES[g], NX)
        hx_send(hbuf.at[slot], slot, 5 + g, xdev[g])
    wz_step(0, 2)
    wz_step(1, 1)
    wz_step(0, 3)
    wz_step(1, 2)
    wz_step(0, 4)
    for g in range(2):
        h_arrived(g * NX + wrap(x + 2, NX), 5 + g)
    load_h.wait()
    wc_wait(0)

    def y_slot(v):
        yy = wrap(v, NY)
        return lax.rem(yy, 2) * 4 + lax.div(yy, 2)

    def y_dot(nh):
        w = wbuf[nh].reshape(KHALF, NHALF)
        h = hbuf[...].reshape(2 * TOK, KHALF)
        for t in range(NHALF // 256):
            part = jnp.dot(h, w[:, t * 256:(t + 1) * 256], preferred_element_type=F32) * SCALE
            yp[nh, :, :, t * 256:(t + 1) * 256] = part.reshape(8, QTOK, 256)

    def y_step(nh, s):
        for side in range(2):
            hops = reach(nh, side, NY)
            if s < hops:
                value = yp[nh, y_slot(y + SIDES[side] * (hops - s))]
                if s:
                    arrived(yrecv.at[nh, side, s - 1], y_s.at[nh, side, s - 1], y_r.at[nh, side, s - 1], ydev[side])
                    value = value + yrecv[nh, side, s - 1].astype(F32)
                ysend[nh, side, s] = value.astype(BF16)
                send(ysend.at[nh, side, s], yrecv.at[nh, side, s], y_s.at[nh, side, s], y_r.at[nh, side, s], ydev[side])

    def stream_place(nh, q):
        return stream_ref.at[pl.ds(pl.multiple_of(q * QTOK, QTOK), QTOK), pl.ds(nh * NHALF, NHALF)]

    stores = []

    def store(src, dst, sem):
        copy = pltpu.make_async_copy(src, dst, sem)
        copy.start()
        stores.append(copy)

    def y_final(nh):
        value = yp[nh, y_slot(y)] + resv[:, nh * NHALF:(nh + 1) * NHALF].astype(F32)
        for side in range(2):
            last = reach(nh, side, NY) - 1
            arrived(yrecv.at[nh, side, last], y_s.at[nh, side, last], y_r.at[nh, side, last], ydev[side])
            value = value + yrecv[nh, side, last].astype(F32)
        yout[nh, yh] = value.astype(BF16)
        for side in range(2):
            send(yout.at[nh, yh], yout.at[nh, yh], ya_s.at[nh, side], ya_r.at[nh, side], y2dev[side])
        store(yout.at[nh, yh], stream_place(nh, yh), loc.at[6 + nh * 4])

    def ya_arrived(nh, k, q):
        arrived(yout.at[nh, q], ya_s.at[nh, k], ya_r.at[nh, k], y2dev[0])

    def y_spread(nh):
        order = (0, 1) if nh == 0 else (1, 0)
        for side in order:
            q = wrap(yh - SIDES[side], 4)
            ya_arrived(nh, side, q)
            if side == nh:
                send(yout.at[nh, q], yout.at[nh, q], ya_s.at[nh, 2], ya_r.at[nh, 2], y2dev[side])
            store(yout.at[nh, q], stream_place(nh, q), loc.at[7 + nh * 4 + side])

    def y_end(nh):
        q = wrap(yh + 2, 4)
        ya_arrived(nh, 2, q)
        store(yout.at[nh, q], stream_place(nh, q), loc.at[9 + nh * 4])

    def h_dot():
        for t in range(2):
            rows = pl.ds(t * 256, 256)
            total = None
            for nh in range(2):
                w = wbuf[nh].reshape(KHALF, NHALF)
                part = lax.dot_general(
                    gbuf[rows, nh * NHALF:(nh + 1) * NHALF], w, (((1,), (1,)), ((), ())),
                    preferred_element_type=F32)
                total = part if total is None else total + part
            hp[t * 4:(t + 1) * 4] = (total * SCALE).reshape(4, QTOK, KHALF)

    def h_step(s):
        for g in range(2):
            for side in range(2):
                hops = reach(g, side, NX)
                if s < hops:
                    value = hp[g * NX + wrap(x + SIDES[side] * (hops - s), NX)]
                    if s:
                        arrived(hrecv.at[g, side, s - 1], dh_s.at[g, side, s - 1], dh_r.at[g, side, s - 1], xdev[side])
                        value = value + hrecv[g, side, s - 1].astype(F32)
                    hsend[g, side, s] = value.astype(BF16)
                    send(hsend.at[g, side, s], hrecv.at[g, side, s], dh_s.at[g, side, s], dh_r.at[g, side, s], xdev[side])

    def h_final():
        for g in range(2):
            value = hp[g * NX + x]
            for side in range(2):
                last = reach(g, side, NX) - 1
                arrived(hrecv.at[g, side, last], dh_s.at[g, side, last], dh_r.at[g, side, last], xdev[side])
                value = value + hrecv[g, side, last].astype(F32)
            hfin[g] = value.astype(BF16)
        send(hfin.at[other], hgrad_ref.at[:, own_cols(yl)], hy_s, hy_r, pdev)
        store(hfin.at[yl], hgrad_ref.at[:, own_cols(yl)], loc.at[14])

    def d_dot():
        h = hbuf[...].reshape(2 * TOK, KHALF)
        for t in range(COLS // 256):
            part = lax.dot_general(
                h, gbuf[:, t * 256:(t + 1) * 256], (((0,), (0,)), ((), ())), preferred_element_type=F32)
            dwp[:, :, t * 256:(t + 1) * 256] = (part * SCALE).reshape(16, ROWS, 256)

    def d_cross():
        for zz in range(NZ):
            dwx_send[zz] = dwp[zz * 2 + 1 - c].astype(BF16)
        send(dwx_send, dwx_recv, dx_s, dx_r, cdev)

    def d_piece(nh, zz):
        cols = slice(nh * NHALF, (nh + 1) * NHALF)
        return dwp[zz * 2 + c, :, cols] + dwx_recv[zz, :, cols].astype(F32)

    def d_step(nh, s):
        for side in range(2):
            hops = reach(nh, side, NZ)
            if s < hops:
                value = d_piece(nh, wrap(z + SIDES[side] * (hops - s), NZ))
                if s:
                    arrived(drecv.at[nh, side, s - 1], dz_s.at[nh, side, s - 1], dz_r.at[nh, side, s - 1], zdev[side])
                    value = value + drecv[nh, side, s - 1].astype(F32)
                dsend[nh, side, s] = value.astype(BF16)
                send(dsend.at[nh, side, s], drecv.at[nh, side, s], dz_s.at[nh, side, s], dz_r.at[nh, side, s], zdev[side])

    def d_final(nh):
        value = d_piece(nh, z)
        for side in range(2):
            last = reach(nh, side, NZ) - 1
            arrived(drecv.at[nh, side, last], dz_s.at[nh, side, last], dz_r.at[nh, side, last], zdev[side])
            value = value + drecv[nh, side, last].astype(F32)
        wgv[:, nh * NHALF:(nh + 1) * NHALF] = value

    def adam():
        grad = wgv[...]
        master = mv[...]
        new_one = beta_one * m1v[...] + (1.0 - beta_one) * grad
        new_two = beta_two * m2v[...] + (1.0 - beta_two) * grad * grad
        bias_one = 1.0 - beta_one**10
        bias_two = 1.0 - beta_two**10
        direction = new_one / bias_one / (jnp.sqrt(new_two / bias_two) + epsilon)
        n1v[...] = new_one
        n2v[...] = new_two
        nmv[...] = master - learn_rate * (direction + weight_decay * master)
        store(wgv, wg_ref, loc.at[15])
        store(nmv, nm_ref, loc.at[16])
        store(n1v, n1_ref, loc.at[17])
        store(n2v, n2_ref, loc.at[18])

    y_dot(0)
    y_step(0, 0)
    wz_step(1, 3)
    wz_step(1, 4)
    load_g.wait()
    arrived(gbuf.at[g_there], gx_s.at[0], gx_r.at[0], hidev)
    arrived(gbuf.at[g_goal], gx_s.at[1], gx_r.at[1], pdev)
    d_dot()
    d_cross()
    y_step(0, 1)
    wc_wait(1)
    y_dot(1)
    y_step(1, 0)
    y_step(0, 2)
    h_dot()
    h_step(0)
    y_step(1, 1)
    arrived(dwx_recv, dx_s, dx_r, cdev)
    for nh in range(2):
        d_step(nh, 0)
    y_step(0, 3)
    h_step(1)
    y_step(1, 2)
    for nh in range(2):
        d_step(nh, 1)
    load_res.wait()
    y_final(0)
    h_final()
    y_step(1, 3)
    for nh in range(2):
        d_step(nh, 2)
    y_final(1)
    y_spread(0)
    for nh in range(2):
        d_step(nh, 3)
    load_m1.wait()
    load_m2.wait()
    y_spread(1)
    for nh in range(2):
        d_final(nh)
    adam()
    y_end(0)
    arrived(hgrad_ref.at[:, own_cols(other)], hy_s, hy_r, pdev)
    y_end(1)
    for copy in stores:
        copy.wait()
    for copy in sent:
        copy.wait_send()


def shards(heads_out, residual, master, moment_one, moment_two, out_grad):
    any_spec = pl.BlockSpec(memory_space=pl.ANY)
    dma = pltpu.SemaphoreType.DMA
    vmem = pltpu.VMEM
    weights = jax.ShapeDtypeStruct((ROWS, COLS), F32)
    outs = pl.pallas_call(
        kernel,
        out_shape=(
            jax.ShapeDtypeStruct((TOK, COLS), BF16),
            jax.ShapeDtypeStruct((QTOK, COLS), BF16),
            weights, weights, weights, weights,
        ),
        in_specs=[any_spec] * 6,
        out_specs=[any_spec] * 6,
        scratch_shapes=[
            vmem((8, QTOK, KHALF), BF16),
            vmem((2 * TOK, COLS), BF16),
            vmem((2, 16, ROWS, NHALF), BF16),
            vmem((2, 8, QTOK, NHALF), F32),
            vmem((2, 2, 4, QTOK, NHALF), BF16),
            vmem((2, 2, 4, QTOK, NHALF), BF16),
            vmem((2, 4, QTOK, NHALF), BF16),
            vmem((QTOK, COLS), BF16),
            vmem((8, QTOK, KHALF), F32),
            vmem((2, 2, 2, QTOK, KHALF), BF16),
            vmem((2, 2, 2, QTOK, KHALF), BF16),
            vmem((2, QTOK, KHALF), BF16),
            vmem((16, ROWS, COLS), F32),
            vmem((8, ROWS, COLS), BF16),
            vmem((8, ROWS, COLS), BF16),
            vmem((2, 2, 4, ROWS, NHALF), BF16),
            vmem((2, 2, 4, ROWS, NHALF), BF16),
            vmem((ROWS, COLS), F32),
            vmem((ROWS, COLS), F32),
            vmem((ROWS, COLS), F32),
            vmem((ROWS, COLS), F32),
            vmem((ROWS, COLS), F32),
            vmem((ROWS, COLS), F32),
            vmem((ROWS, COLS), F32),
            dma((2, 2, 4)), dma((2, 2, 4)), dma((2, 8)), dma((2, 8)),
            dma((7,)), dma((7,)), dma((2,)), dma((2,)),
            dma((2, 2, 4)), dma((2, 2, 4)), dma((2, 3)), dma((2, 3)),
            dma((2, 2, 2)), dma((2, 2, 2)), dma, dma, dma, dma,
            dma((2, 2, 4)), dma((2, 2, 4)), dma((19,)),
        ],
        compiler_params=pltpu.CompilerParams(
            collective_id=0, has_side_effects=True, vmem_limit_bytes=48 << 20),
        cost_estimate=pl.CostEstimate(
            flops=6 * TOK * COLS * COLS, bytes_accessed=5 << 20, transcendentals=ROWS * COLS),
    )(heads_out, residual, master, moment_one, moment_two, out_grad)
    return tuple(outs)


def solution(mesh):
    return jax.shard_map(
        shards,
        mesh=mesh,
        in_specs=(
            P(("dp", "col"), "row"),
            P("dp", "col"),
            P(("row", "dp"), "col"),
            P(("row", "dp"), "col"),
            P(("row", "dp"), "col"),
            P("dp", "col"),
        ),
        out_specs=(
            P("dp", "col"),
            P(("dp", "col"), "row"),
            P(("row", "dp"), "col"),
            P(("row", "dp"), "col"),
            P(("row", "dp"), "col"),
            P(("row", "dp"), "col"),
        ),
        check_vma=False,
    )
```

time: 277 us -> 85.2 us (0.31)
  the two profiles are of different devices: /device:TPU:4 before, /device:TPU:2 now
where the time goes in v1:
time: 85.2 us; the launch traced here: 84.8 us
  Pallas kernels  73.7 us (87%)
  local copies, waits for them, and re-layouts  10.5 us (12%)
    pallas_call x1, Pallas kernels, shards(): pl.pallas_call(kernel, out_shape=(jax.ShapeDtypeStruct((TOK, COLS), BF16)...  73.7 us
    unnamed x18, local copies, waits for them, and re-layouts  10.5 us

profile of v1, /device:TPU:2, one launch (start us, length us, event | category | flops | bytes accessed | tf_op | source)
XLA Modules:
  0.0 84.8 jit_solution(18281411593643451769)
XLA Ops:
  0.6 0.0 copy-start
  0.6 1.1 %copy-done = bf16[256,1536]{1,0:T(8,128)(2,1)S(1)} copy-done((bf16[256,1536]{1,0:T(8,128)(2,1)S(1)}, bf16[256,1536]{1,0:T(8,128)(2,1)}, u32[]{:S(2)}) %copy-start) | copy-done | bytes 786456
  1.8 0.0 copy-start.1
  1.8 1.1 %copy-done.1 = bf16[256,1536]{1,0:T(8,128)(2,1)S(1)} copy-done((bf16[256,1536]{1,0:T(8,128)(2,1)S(1)}, bf16[256,1536]{1,0:T(8,128)(2,1)}, u32[]{:S(2)}) %copy-start.1) | copy-done | bytes 786456
  2.9 0.0 copy-start.2
  2.9 1.0 %copy-done.2 = f32[48,1536]{1,0:T(8,128)S(1)} copy-done((f32[48,1536]{1,0:T(8,128)S(1)}, f32[48,1536]{1,0:T(8,128)}, u32[]{:S(2)}) %copy-start.2) | copy-done | bytes 294936
  3.9 0.0 copy-start.3
  3.9 1.0 %copy-done.3 = f32[48,1536]{1,0:T(8,128)S(1)} copy-done((f32[48,1536]{1,0:T(8,128)S(1)}, f32[48,1536]{1,0:T(8,128)}, u32[]{:S(2)}) %copy-start.3) | copy-done | bytes 294936
  4.8 0.0 copy-start.4
  4.8 1.0 %copy-done.4 = f32[48,1536]{1,0:T(8,128)S(1)} copy-done((f32[48,1536]{1,0:T(8,128)S(1)}, f32[48,1536]{1,0:T(8,128)}, u32[]{:S(2)}) %copy-start.4) | copy-done | bytes 294936
  5.8 0.0 copy-start.5
  5.8 0.9 %copy-done.5 = bf16[64,1536]{1,0:T(8,128)(2,1)S(1)} copy-done((bf16[64,1536]{1,0:T(8,128)(2,1)S(1)}, bf16[64,1536]{1,0:T(8,128)(2,1)}, u32[]{:S(2)}) %copy-start.5) | copy-done | bytes 196632
  6.7 73.7 %shard_map.109 = (bf16[256,1536]{1,0:T(8,128)(2,1)S(1)}, bf16[64,1536]{1,0:T(8,128)(2,1)S(1)}, f32[48,1536]{1,0:T(8,128)S(1)}, f32[48,1536]{1,0:T(8,128)S(1)}, f...) custom-call(bf16[64,1536]{1,0:T(8,128)(2,1)S(1)} %copy-done.5, bf16[256,1536]{1,0:T(8,128)(2,1)S(1)} %copy-done, ...), custom_call_target="tpu_custom_call" | custom-call | flops 3623878656 | bytes 5242880 | tf_op jit(solution)/shard_map/pallas_call | solution.py:382
  80.4 0.9 %copy.18 = bf16[256,1536]{1,0:T(8,128)(2,1)} copy(bf16[256,1536]{1,0:T(8,128)(2,1)S(1)} %get-tuple-element.12) | data formatting | bytes 1572864
  81.3 0.7 copy.19
  82.0 0.7 copy.20
  82.7 0.7 copy.21
  83.4 0.7 copy.22
  84.1 0.7 copy.23
Async XLA Ops:
  0.6 1.1 %copy-start = (bf16[256,1536]{1,0:T(8,128)(2,1)S(1)}, bf16[256,1536]{1,0:T(8,128)(2,1)}, u32[]{:S(2)}) copy-start(bf16[256,1536]{1,0:T(8,128)(2,1)} %res_ref.1) | copy-start | bytes 2359300
  1.8 1.1 %copy-start.1 = (bf16[256,1536]{1,0:T(8,128)(2,1)S(1)}, bf16[256,1536]{1,0:T(8,128)(2,1)}, u32[]{:S(2)}) copy-start(bf16[256,1536]{1,0:T(8,128)(2,1)} %g_ref.1) | copy-start | bytes 2359300
  2.9 1.0 %copy-start.2 = (f32[48,1536]{1,0:T(8,128)S(1)}, f32[48,1536]{1,0:T(8,128)}, u32[]{:S(2)}) copy-start(f32[48,1536]{1,0:T(8,128)} %master_ref.1) | copy-start | bytes 884740
  3.9 1.0 %copy-start.3 = (f32[48,1536]{1,0:T(8,128)S(1)}, f32[48,1536]{1,0:T(8,128)}, u32[]{:S(2)}) copy-start(f32[48,1536]{1,0:T(8,128)} %m1_ref.1) | copy-start | bytes 884740
  4.8 1.0 %copy-start.4 = (f32[48,1536]{1,0:T(8,128)S(1)}, f32[48,1536]{1,0:T(8,128)}, u32[]{:S(2)}) copy-start(f32[48,1536]{1,0:T(8,128)} %m2_ref.1) | copy-start | bytes 884740
  5.8 0.9 %copy-start.5 = (bf16[64,1536]{1,0:T(8,128)(2,1)S(1)}, bf16[64,1536]{1,0:T(8,128)(2,1)}, u32[]{:S(2)}) copy-start(bf16[64,1536]{1,0:T(8,128)(2,1)} %h_ref.1) | copy-start | bytes 589828

commit v2 on v1

v2 whole, which is shorter than its diff:
```python
import math

import jax
import jax.numpy as jnp
from jax import lax
from jax.experimental import pallas as pl
from jax.experimental.pallas import tpu as pltpu
from jax.sharding import PartitionSpec as P

HEADS = 48
HEAD_DIM = 128

beta_one = 0.9
beta_two = 0.95
learn_rate = 0.1
weight_decay = 0.1
epsilon = 1e-08

MESH = pl.DeviceIdType.MESH
BF16, F32 = jnp.bfloat16, jnp.float32

NX, NY, NZ = 4, 8, 8
TOK = 256
QTOK = 64
KHALF = 768
COLS = 1536
NHALF = 768
PARTS = 4
WIDE = COLS // PARTS
ROWS = 48
SIDES = (1, -1)
SCALE = 1.0 / math.sqrt(HEADS * HEAD_DIM)


def reach(part, side, around):
    longer = around // 2
    return longer if part % 2 == side else around - 1 - longer


def kernel(
    h_ref, res_ref, master_ref, m1_ref, m2_ref, g_ref,
    yout, hgrad, wgv, nmv, n1v, n2v,
    hbuf, gbuf, wbuf, yp, ysend, yrecv, resv,
    hp, hsend, hrecv, hfin, dwp, dwx_send, dwx_recv, dsend, drecv,
    mv, m1v, m2v,
    wz_s, wz_r, wc_s, wc_r, hx_s, hx_r, gx_s, gx_r, y_s, y_r, ya_s, ya_r,
    dh_s, dh_r, hy_s, hy_r, dx_s, dx_r, dz_s, dz_r, loc,
):
    dp, yh, x = lax.axis_index("dp"), lax.axis_index("row"), lax.axis_index("col")
    c = lax.rem(dp, 2)
    z = lax.rem(lax.div(dp, 2), NZ)
    yl = lax.div(dp, 2 * NZ)
    y = 2 * yh + yl

    def wrap(v, n):
        return lax.rem(v + n, n)

    def device(dx=0, dy=0, dz=0, flip=False):
        yy = wrap(y + dy, NY)
        core = 1 - c if flip else c
        return ((lax.rem(yy, 2) * NZ + wrap(z + dz, NZ)) * 2 + core, lax.div(yy, 2), wrap(x + dx, NX))

    to_partner = 1 - 2 * yl
    zdev = [device(dz=s) for s in SIDES]
    xdev = [device(dx=s) for s in SIDES]
    ydev = [device(dy=s) for s in SIDES]
    y2dev = [device(dy=2 * s) for s in SIDES]
    cdev = device(flip=True)
    pdev = device(dy=to_partner)
    hidev = device(dy=-to_partner)

    sent = []

    def remote(src, dst, ssem, rsem, dev):
        return pltpu.make_async_remote_copy(
            src_ref=src, dst_ref=dst, send_sem=ssem, recv_sem=rsem, device_id=dev, device_id_type=MESH)

    def send(src, dst, ssem, rsem, dev):
        copy = remote(src, dst, ssem, rsem, dev)
        copy.start()
        sent.append(copy)

    def arrived(dst, ssem, rsem, dev):
        remote(dst, dst, ssem, rsem, dev).wait_recv()

    def own_cols(v):
        return pl.ds(pl.multiple_of(v * KHALF, KHALF), KHALF)

    load_master = pltpu.make_async_copy(master_ref, mv, loc.at[0])
    load_master.start()
    load_h = pltpu.make_async_copy(h_ref.at[:, own_cols(yl)], hbuf.at[yl * NX + x], loc.at[1])
    load_h.start()
    load_g = pltpu.make_async_copy(g_ref, gbuf.at[pl.ds(pl.multiple_of(yl * TOK, TOK), TOK)], loc.at[2])
    load_g.start()
    load_res = pltpu.make_async_copy(
        res_ref.at[pl.ds(pl.multiple_of(yh * QTOK, QTOK), QTOK)], resv, loc.at[3])
    load_res.start()
    load_m1 = pltpu.make_async_copy(m1_ref, m1v, loc.at[4])
    load_m1.start()
    load_m2 = pltpu.make_async_copy(m2_ref, m2v, loc.at[5])
    load_m2.start()

    def wz_send(n, side, s):
        slot = wbuf.at[n, wrap(z - SIDES[side] * s, NZ) * 2 + c]
        send(slot, slot, wz_s.at[n, side, s], wz_r.at[n, side, s], zdev[side])

    def wc_send(n, k, zz):
        slot = wbuf.at[n, zz * 2 + c]
        send(slot, slot, wc_s.at[n, k], wc_r.at[n, k], cdev)

    def wz_step(n, s):
        for side in range(2):
            if s <= reach(n, side, NZ):
                zz = wrap(z - SIDES[side] * s, NZ)
                arrived(wbuf.at[n, zz * 2 + c], wz_s.at[n, side, s - 1], wz_r.at[n, side, s - 1], zdev[side])
                if s < reach(n, side, NZ):
                    wz_send(n, side, s)
                wc_send(n, s if side == 0 else reach(n, 0, NZ) + s, zz)

    def wc_wait(n):
        for k in range(NZ):
            up = reach(n, 0, NZ)
            zz = z if k == 0 else wrap(z - k, NZ) if k <= up else wrap(z + (k - up), NZ)
            arrived(wbuf.at[n, zz * 2 + 1 - c], wc_s.at[n, k], wc_r.at[n, k], cdev)

    other = 1 - yl
    half = TOK // 2
    g_first = pl.ds(pl.multiple_of(other * half, half), half)
    g_there = pl.ds(pl.multiple_of(yl * TOK + other * half, half), half)
    g_last = pl.ds(pl.multiple_of(yl * half, half), half)
    g_goal = pl.ds(pl.multiple_of(yl * TOK + yl * half, half), half)

    def hx_send(src, slot, k, dev):
        send(src, hbuf.at[slot], hx_s.at[k], hx_r.at[k], dev)

    def h_arrived(slot, k):
        arrived(hbuf.at[slot], hx_s.at[k], hx_r.at[k], pdev)

    def h_far(g, k):
        step = 1 - 2 * g
        slot = g * NX + wrap(x - step, NX)
        hx_send(hbuf.at[slot], slot, k, device(dx=step))

    def y_slot(v):
        yy = wrap(v, NY)
        return lax.rem(yy, 2) * 4 + lax.div(yy, 2)

    def y_dot(n):
        h = hbuf[...].reshape(2 * TOK, KHALF)
        part = jnp.dot(h, wbuf[n].reshape(KHALF, WIDE), preferred_element_type=F32) * SCALE
        yp[n] = part.reshape(8, QTOK, WIDE)

    def y_step(n, s):
        for side in range(2):
            hops = reach(n, side, NY)
            if s < hops:
                value = yp[n, y_slot(y + SIDES[side] * (hops - s))]
                if s:
                    arrived(yrecv.at[n, side, s - 1], y_s.at[n, side, s - 1], y_r.at[n, side, s - 1], ydev[side])
                    value = value + yrecv[n, side, s - 1].astype(F32)
                ysend[n, side, s] = value.astype(BF16)
                send(ysend.at[n, side, s], yrecv.at[n, side, s], y_s.at[n, side, s], y_r.at[n, side, s], ydev[side])

    def y_final(n):
        value = yp[n, y_slot(y)] + resv[:, n * WIDE:(n + 1) * WIDE].astype(F32)
        for side in range(2):
            last = reach(n, side, NY) - 1
            arrived(yrecv.at[n, side, last], y_s.at[n, side, last], y_r.at[n, side, last], ydev[side])
            value = value + yrecv[n, side, last].astype(F32)
        yout[n, yh] = value.astype(BF16)
        for side in range(2):
            send(yout.at[n, yh], yout.at[n, yh], ya_s.at[n, side], ya_r.at[n, side], y2dev[side])

    def ya_arrived(n, k, q):
        arrived(yout.at[n, q], ya_s.at[n, k], ya_r.at[n, k], y2dev[0])

    def y_spread(n):
        order = (0, 1) if n % 2 == 0 else (1, 0)
        for side in order:
            q = wrap(yh - SIDES[side], 4)
            ya_arrived(n, side, q)
            if side == n % 2:
                send(yout.at[n, q], yout.at[n, q], ya_s.at[n, 2], ya_r.at[n, 2], y2dev[side])

    def y_end(n):
        q = wrap(yh + 2, 4)
        ya_arrived(n, 2, q)

    def h_dot():
        for t in range(2):
            rows = pl.ds(t * 256, 256)
            total = None
            for n in range(PARTS):
                w = wbuf[n].reshape(KHALF, WIDE)
                part = lax.dot_general(
                    gbuf[rows, n * WIDE:(n + 1) * WIDE], w, (((1,), (1,)), ((), ())),
                    preferred_element_type=F32)
                total = part if total is None else total + part
            hp[t * 4:(t + 1) * 4] = (total * SCALE).reshape(4, QTOK, KHALF)

    def h_step(s):
        for g in range(2):
            for side in range(2):
                hops = reach(g, side, NX)
                if s < hops:
                    value = hp[g * NX + wrap(x + SIDES[side] * (hops - s), NX)]
                    if s:
                        arrived(hrecv.at[g, side, s - 1], dh_s.at[g, side, s - 1], dh_r.at[g, side, s - 1], xdev[side])
                        value = value + hrecv[g, side, s - 1].astype(F32)
                    hsend[g, side, s] = value.astype(BF16)
                    send(hsend.at[g, side, s], hrecv.at[g, side, s], dh_s.at[g, side, s], dh_r.at[g, side, s], xdev[side])

    def h_final():
        for g in range(2):
            value = hp[g * NX + x]
            for side in range(2):
                last = reach(g, side, NX) - 1
                arrived(hrecv.at[g, side, last], dh_s.at[g, side, last], dh_r.at[g, side, last], xdev[side])
                value = value + hrecv[g, side, last].astype(F32)
            hfin[g] = value.astype(BF16)
        send(hfin.at[other], hgrad.at[yl], hy_s, hy_r, pdev)
        hgrad[yl] = hfin[yl]

    def d_dot():
        h = hbuf[...].reshape(2 * TOK, KHALF)
        for t in range(COLS // 256):
            part = lax.dot_general(
                h, gbuf[:, t * 256:(t + 1) * 256], (((0,), (0,)), ((), ())), preferred_element_type=F32)
            dwp[:, :, t * 256:(t + 1) * 256] = (part * SCALE).reshape(16, ROWS, 256)

    def d_cross():
        for zz in range(NZ):
            dwx_send[zz] = dwp[zz * 2 + 1 - c].astype(BF16)
        send(dwx_send, dwx_recv, dx_s, dx_r, cdev)

    def d_piece(nh, zz):
        cols = slice(nh * NHALF, (nh + 1) * NHALF)
        return dwp[zz * 2 + c, :, cols] + dwx_recv[zz, :, cols].astype(F32)

    def d_step(nh, s):
        for side in range(2):
            hops = reach(nh, side, NZ)
            if s < hops:
                value = d_piece(nh, wrap(z + SIDES[side] * (hops - s), NZ))
                if s:
                    arrived(drecv.at[nh, side, s - 1], dz_s.at[nh, side, s - 1], dz_r.at[nh, side, s - 1], zdev[side])
                    value = value + drecv[nh, side, s - 1].astype(F32)
                dsend[nh, side, s] = value.astype(BF16)
                send(dsend.at[nh, side, s], drecv.at[nh, side, s], dz_s.at[nh, side, s], dz_r.at[nh, side, s], zdev[side])

    def d_final(nh):
        value = d_piece(nh, z)
        for side in range(2):
            last = reach(nh, side, NZ) - 1
            arrived(drecv.at[nh, side, last], dz_s.at[nh, side, last], dz_r.at[nh, side, last], zdev[side])
            value = value + drecv[nh, side, last].astype(F32)
        wgv[:, nh * NHALF:(nh + 1) * NHALF] = value

    def adam():
        grad = wgv[...]
        master = mv[...]
        new_one = beta_one * m1v[...] + (1.0 - beta_one) * grad
        new_two = beta_two * m2v[...] + (1.0 - beta_two) * grad * grad
        bias_one = 1.0 - beta_one**10
        bias_two = 1.0 - beta_two**10
        direction = new_one / bias_one / (jnp.sqrt(new_two / bias_two) + epsilon)
        n1v[...] = new_one
        n2v[...] = new_two
        nmv[...] = master - learn_rate * (direction + weight_decay * master)

    barrier = pltpu.get_barrier_semaphore()
    around = zdev + xdev + ydev + y2dev + [cdev]
    for dev in around:
        pl.semaphore_signal(barrier, inc=1, device_id=dev, device_id_type=MESH)
    load_master.wait()
    own = z * 2 + c
    for n in range(PARTS):
        wbuf[n, own] = mv[:, n * WIDE:(n + 1) * WIDE].astype(BF16)
    pl.semaphore_wait(barrier, len(around))

    for side in range(2):
        wz_send(0, side, 0)
    hx_send(h_ref.at[:, own_cols(other)], yl * NX + x, 0, pdev)
    for side in range(2):
        hx_send(h_ref.at[:, own_cols(yl)], yl * NX + x, 1 + side, xdev[side])
    wc_send(0, 0, z)
    for side in range(2):
        wz_send(1, side, 0)
    send(g_ref.at[g_first], gbuf.at[g_there], gx_s.at[0], gx_r.at[0], hidev)
    wc_send(1, 0, z)
    for n in range(2, PARTS):
        for side in range(2):
            wz_send(n, side, 0)
        wc_send(n, 0, z)

    wz_step(0, 1)
    wz_step(1, 1)
    h_arrived(other * NX + x, 0)
    for side in range(2):
        hx_send(hbuf.at[other * NX + x], other * NX + x, 3 + side, xdev[side])
    send(g_ref.at[g_last], gbuf.at[g_goal], gx_s.at[1], gx_r.at[1], pdev)
    wz_step(2, 1)
    wz_step(3, 1)
    for side in range(2):
        h_arrived(yl * NX + wrap(x - SIDES[side], NX), 1 + side)
    h_far(yl, 5)
    wz_step(0, 2)
    wz_step(1, 2)
    wz_step(2, 2)
    for side in range(2):
        h_arrived(other * NX + wrap(x - SIDES[side], NX), 3 + side)
    h_far(other, 6)
    wz_step(3, 2)
    for n in range(PARTS):
        wz_step(n, 3)
    wz_step(0, 4)
    load_h.wait()
    h_arrived(yl * NX + wrap(x + 2, NX), 5)
    h_arrived(other * NX + wrap(x + 2, NX), 6)
    wc_wait(0)
    y_dot(0)
    y_step(0, 0)
    wz_step(1, 4)
    wz_step(2, 4)
    wz_step(3, 4)
    wc_wait(1)
    y_dot(1)
    y_step(1, 0)
    wc_wait(2)
    y_dot(2)
    y_step(2, 0)
    y_step(0, 1)
    wc_wait(3)
    y_dot(3)
    y_step(3, 0)
    load_g.wait()
    arrived(gbuf.at[g_there], gx_s.at[0], gx_r.at[0], hidev)
    arrived(gbuf.at[g_goal], gx_s.at[1], gx_r.at[1], pdev)
    y_step(1, 1)
    d_dot()
    d_cross()
    y_step(2, 1)
    y_step(0, 2)
    y_step(3, 1)
    h_dot()
    h_step(0)
    y_step(1, 2)
    y_step(2, 2)
    arrived(dwx_recv, dx_s, dx_r, cdev)
    for nh in range(2):
        d_step(nh, 0)
    y_step(0, 3)
    y_step(3, 2)
    y_step(1, 3)
    h_step(1)
    y_step(2, 3)
    load_res.wait()
    y_final(0)
    for nh in range(2):
        d_step(nh, 1)
    y_step(3, 3)
    y_final(1)
    y_final(2)
    h_final()
    y_spread(0)
    for nh in range(2):
        d_step(nh, 2)
    y_final(3)
    y_spread(1)
    y_spread(2)
    for nh in range(2):
        d_step(nh, 3)
    load_m1.wait()
    load_m2.wait()
    y_spread(3)
    for nh in range(2):
        d_final(nh)
    adam()
    arrived(hgrad.at[other], hy_s, hy_r, pdev)
    for n in range(PARTS):
        y_end(n)
    for copy in sent:
        copy.wait_send()


def hand_over(yout, hgrad, *refs):
    weights, stream, heads, outs, sems = refs[:4], refs[4], refs[5], refs[6:10], refs[10]
    pairs = list(zip(weights, outs))
    for half in range(2):
        pairs.append((hgrad.at[half], heads.at[:, pl.ds(half * KHALF, KHALF)]))
    for n in range(PARTS):
        for q in range(4):
            pairs.append((yout.at[n, q], stream.at[pl.ds(q * QTOK, QTOK), pl.ds(n * WIDE, WIDE)]))
    copies = [pltpu.make_async_copy(src, dst, sems.at[i]) for i, (src, dst) in enumerate(pairs)]
    for copy in copies:
        copy.start()
    for copy in copies:
        copy.wait()


def shards(heads_out, residual, master, moment_one, moment_two, out_grad):
    any_spec = pl.BlockSpec(memory_space=pl.ANY)
    dma = pltpu.SemaphoreType.DMA
    vmem = pltpu.VMEM
    weights = pltpu.VMEM((ROWS, COLS), F32)
    outs = pl.pallas_call(
        kernel,
        out_shape=(
            vmem((PARTS, 4, QTOK, WIDE), BF16),
            vmem((2, QTOK, KHALF), BF16),
            weights, weights, weights, weights,
        ),
        in_specs=[any_spec] * 6,
        out_specs=[pl.BlockSpec(memory_space=vmem)] * 6,
        scratch_shapes=[
            vmem((8, QTOK, KHALF), BF16),
            vmem((2 * TOK, COLS), BF16),
            vmem((PARTS, 16, ROWS, WIDE), BF16),
            vmem((PARTS, 8, QTOK, WIDE), F32),
            vmem((PARTS, 2, 4, QTOK, WIDE), BF16),
            vmem((PARTS, 2, 4, QTOK, WIDE), BF16),
            vmem((QTOK, COLS), BF16),
            vmem((8, QTOK, KHALF), F32),
            vmem((2, 2, 2, QTOK, KHALF), BF16),
            vmem((2, 2, 2, QTOK, KHALF), BF16),
            vmem((2, QTOK, KHALF), BF16),
            vmem((16, ROWS, COLS), F32),
            vmem((8, ROWS, COLS), BF16),
            vmem((8, ROWS, COLS), BF16),
            vmem((2, 2, 4, ROWS, NHALF), BF16),
            vmem((2, 2, 4, ROWS, NHALF), BF16),
            vmem((ROWS, COLS), F32),
            vmem((ROWS, COLS), F32),
            vmem((ROWS, COLS), F32),
            dma((PARTS, 2, 4)), dma((PARTS, 2, 4)), dma((PARTS, 8)), dma((PARTS, 8)),
            dma((7,)), dma((7,)), dma((2,)), dma((2,)),
            dma((PARTS, 2, 4)), dma((PARTS, 2, 4)), dma((PARTS, 3)), dma((PARTS, 3)),
            dma((2, 2, 2)), dma((2, 2, 2)), dma, dma, dma, dma,
            dma((2, 2, 4)), dma((2, 2, 4)), dma((6,)),
        ],
        compiler_params=pltpu.CompilerParams(
            collective_id=0, has_side_effects=True, vmem_limit_bytes=40 << 20),
        cost_estimate=pl.CostEstimate(
            flops=6 * TOK * COLS * COLS, bytes_accessed=5 << 20, transcendentals=ROWS * COLS),
    )(*(pltpu.with_memory_space_constraint(v, pltpu.HBM)
        for v in (heads_out, residual, master, moment_one, moment_two, out_grad)))
    return tuple(pl.pallas_call(
        hand_over,
        out_shape=[pltpu.HBM((TOK, COLS), BF16), pltpu.HBM((QTOK, COLS), BF16)] + [pltpu.HBM((ROWS, COLS), F32)] * 4,
        in_specs=[any_spec] * 6,
        out_specs=[any_spec] * 6,
        scratch_shapes=[dma((6 + 4 * PARTS,))],
        compiler_params=pltpu.CompilerParams(vmem_limit_bytes=8 << 20),
    )(*outs))


def solution(mesh):
    return jax.shard_map(
        shards,
        mesh=mesh,
        in_specs=(
            P(("dp", "col"), "row"),
            P("dp", "col"),
            P(("row", "dp"), "col"),
            P(("row", "dp"), "col"),
            P(("row", "dp"), "col"),
            P("dp", "col"),
        ),
        out_specs=(
            P("dp", "col"),
            P(("dp", "col"), "row"),
            P(("row", "dp"), "col"),
            P(("row", "dp"), "col"),
            P(("row", "dp"), "col"),
            P(("row", "dp"), "col"),
        ),
        check_vma=False,
    )
```

time: 85.2 us -> 68.2 us (0.80)
  the two profiles are of different devices: /device:TPU:2 before, /device:TPU:8 now
where the time goes in v2:
time: 68.2 us; the launch traced here: 68 us
  Pallas kernels  67.4 us (99%)
    pallas_call x1, Pallas kernels, shards(): pl.pallas_call(kernel, out_shape=(vmem((PARTS, 4, QTOK, WIDE), BF16), vme...  65.9 us
    pallas_call x1, Pallas kernels, shards(): pl.pallas_call(hand_over, out_shape=[pltpu.HBM((TOK, COLS), BF16), pltpu....  1.51 us

profile of v2, /device:TPU:8, one launch (start us, length us, event | category | flops | bytes accessed | tf_op | source)
XLA Modules:
  0.0 68.0 jit_solution(1480433929049306271)
XLA Ops:
  0.6 65.9 %shard_map.109 = (bf16[4,4,64,384]{3,2,1,0:T(8,128)(2,1)S(1)}, bf16[2,64,768]{2,1,0:T(8,128)(2,1)S(1)}, f32[48,1536]{1,0:T(8,128)S(1)}, f32[48,1536]{1,0:T(8,128...) custom-call(bf16[64,1536]{1,0:T(8,128)(2,1)} %h_ref.1, bf16[256,1536]{1,0:T(8,128)(2,1)} %res_ref.1, ...), custom_call_target="tpu_custom_call" | custom-call | flops 3623878656 | bytes 5242880 | tf_op jit(solution)/shard_map/pallas_call | solution.py:406
  66.5 1.5 %shard_map.110 = (bf16[256,1536]{1,0:T(8,128)(2,1)}, bf16[64,1536]{1,0:T(8,128)(2,1)}, f32[48,1536]{1,0:T(8,128)}, f32[48,1536]{1,0:T(8,128)}, f32[48,1536]{1,0:T(8,128)}, /*index=5*/f32[48,1536]{1,0:T(8,128)}) custom-call(bf16[4,4,64,384]{3,2,1,0:T(8,128)(2,1)S(1)} %get-tuple-element.12.yout, bf16[2,64,768]{2,1,0:T(8,128)(2,1)S(1)} %get-tuple-element.13.hgrad, ...), custom_call_target="tpu_custom_call" | custom-call | tf_op jit(solution)/shard_map/pallas_call | solution.py:447

commit v3 on v2

--- a/solution.py
+++ b/solution.py
@@ -231,7 +231,7 @@
     def d_cross():
         for zz in range(NZ):
             dwx_send[zz] = dwp[zz * 2 + 1 - c].astype(BF16)
-        send(dwx_send, dwx_recv, dx_s, dx_r, cdev)
+            send(dwx_send.at[zz], dwx_recv.at[zz], dx_s.at[zz], dx_r.at[zz], cdev)
 
     def d_piece(nh, zz):
         cols = slice(nh * NHALF, (nh + 1) * NHALF)
@@ -283,27 +283,26 @@
     hx_send(h_ref.at[:, own_cols(other)], yl * NX + x, 0, pdev)
     for side in range(2):
         hx_send(h_ref.at[:, own_cols(yl)], yl * NX + x, 1 + side, xdev[side])
-    wc_send(0, 0, z)
     for side in range(2):
         wz_send(1, side, 0)
-    send(g_ref.at[g_first], gbuf.at[g_there], gx_s.at[0], gx_r.at[0], hidev)
-    wc_send(1, 0, z)
     for n in range(2, PARTS):
         for side in range(2):
             wz_send(n, side, 0)
+
+    for n in range(PARTS):
         wc_send(n, 0, z)
-
     wz_step(0, 1)
     wz_step(1, 1)
     h_arrived(other * NX + x, 0)
     for side in range(2):
         hx_send(hbuf.at[other * NX + x], other * NX + x, 3 + side, xdev[side])
-    send(g_ref.at[g_last], gbuf.at[g_goal], gx_s.at[1], gx_r.at[1], pdev)
+    send(g_ref.at[g_first], gbuf.at[g_there], gx_s.at[0], gx_r.at[0], hidev)
     wz_step(2, 1)
     wz_step(3, 1)
     for side in range(2):
         h_arrived(yl * NX + wrap(x - SIDES[side], NX), 1 + side)
     h_far(yl, 5)
+    send(g_ref.at[g_last], gbuf.at[g_goal], gx_s.at[1], gx_r.at[1], pdev)
     wz_step(0, 2)
     wz_step(1, 2)
     wz_step(2, 2)
@@ -342,30 +341,31 @@
     y_step(2, 1)
     y_step(0, 2)
     y_step(3, 1)
+    y_step(1, 2)
+    y_step(2, 2)
+    for zz in range(NZ):
+        arrived(dwx_recv.at[zz], dx_s.at[zz], dx_r.at[zz], cdev)
+    for nh in range(2):
+        d_step(nh, 0)
     h_dot()
     h_step(0)
-    y_step(1, 2)
-    y_step(2, 2)
-    arrived(dwx_recv, dx_s, dx_r, cdev)
-    for nh in range(2):
-        d_step(nh, 0)
     y_step(0, 3)
     y_step(3, 2)
     y_step(1, 3)
-    h_step(1)
     y_step(2, 3)
     load_res.wait()
     y_final(0)
     for nh in range(2):
         d_step(nh, 1)
     y_step(3, 3)
+    h_step(1)
     y_final(1)
     y_final(2)
-    h_final()
     y_spread(0)
     for nh in range(2):
         d_step(nh, 2)
     y_final(3)
+    h_final()
     y_spread(1)
     y_spread(2)
     for nh in range(2):
@@ -435,7 +435,7 @@
             dma((PARTS, 2, 4)), dma((PARTS, 2, 4)), dma((PARTS, 8)), dma((PARTS, 8)),
             dma((7,)), dma((7,)), dma((2,)), dma((2,)),
             dma((PARTS, 2, 4)), dma((PARTS, 2, 4)), dma((PARTS, 3)), dma((PARTS, 3)),
-            dma((2, 2, 2)), dma((2, 2, 2)), dma, dma, dma, dma,
+            dma((2, 2, 2)), dma((2, 2, 2)), dma, dma, dma((8,)), dma((8,)),
             dma((2, 2, 4)), dma((2, 2, 4)), dma((6,)),
         ],
         compiler_params=pltpu.CompilerParams(

time: 68.2 us -> 67.6 us (level)
  no operation moved by 1% of the time
where the time goes in v3:
time: 67.6 us; the launch traced here: 67.5 us
  Pallas kernels  66.8 us (99%)
    pallas_call x1, Pallas kernels, shards(): pl.pallas_call(kernel, out_shape=(vmem((PARTS, 4, QTOK, WIDE), BF16), vme...  65.3 us
    pallas_call x1, Pallas kernels, shards(): pl.pallas_call(hand_over, out_shape=[pltpu.HBM((TOK, COLS), BF16), pltpu....  1.51 us

profile of v3, /device:TPU:8, one launch (start us, length us, event | category | flops | bytes accessed | tf_op | source)
XLA Modules:
  0.0 67.5 jit_solution(3284466110738005429)
XLA Ops:
  0.6 65.3 %shard_map.109 = (bf16[4,4,64,384]{3,2,1,0:T(8,128)(2,1)S(1)}, bf16[2,64,768]{2,1,0:T(8,128)(2,1)S(1)}, f32[48,1536]{1,0:T(8,128)S(1)}, f32[48,1536]{1,0:T(8,128...) custom-call(bf16[64,1536]{1,0:T(8,128)(2,1)} %h_ref.1, bf16[256,1536]{1,0:T(8,128)(2,1)} %res_ref.1, ...), custom_call_target="tpu_custom_call" | custom-call | flops 3623878656 | bytes 5242880 | tf_op jit(solution)/shard_map/pallas_call | solution.py:406
  66.0 1.5 %shard_map.110 = (bf16[256,1536]{1,0:T(8,128)(2,1)}, bf16[64,1536]{1,0:T(8,128)(2,1)}, f32[48,1536]{1,0:T(8,128)}, f32[48,1536]{1,0:T(8,128)}, f32[48,1536]{1,0:T(8,128)}, /*index=5*/f32[48,1536]{1,0:T(8,128)}) custom-call(bf16[4,4,64,384]{3,2,1,0:T(8,128)(2,1)S(1)} %get-tuple-element.12.yout, bf16[2,64,768]{2,1,0:T(8,128)(2,1)S(1)} %get-tuple-element.13.hgrad, ...), custom_call_target="tpu_custom_call" | custom-call | tf_op jit(solution)/shard_map/pallas_call | solution.py:447
